TPU v7x, 256 devices: a whole 4x4x8 slice. The times are simulated.
256 devices in a mesh: row: 32 (over x, y, core), col: 8 (over z).
Axes of the slice: x: 4, y: 4, z: 8, core: 2. Of those that a mesh axis runs over, the one named last changes fastest.
Arguments:
- source: bfloat16 [32768, 128], P(('row', 'col')), may hold values from -10 to 10
- target: bfloat16 [32768, 128], P(('col', 'row')), may hold values from -80 to 80
- target_potential: bfloat16 [32768], P(('col', 'row')), may hold values from -4 to 4
- prev_moment: float32 [128, 128], replicated, may hold values from -0.1 to 0.5
Outputs:
- moment: float32 [128, 128], replicated
- source_potential: float32 [32768], P('row')
- target_update: float32 [32768], P(('col', 'row'))
All inputs are finite; a program needn't handle non-finite values.
Results may differ from a plain program's by a relative error of at most 0.0059.
Values may be sent and summed in bfloat16 or wider, within the bound.
A program may use at most 64 MiB of HBM per device.

v0:
```python
import math
import jax
import jax.numpy as jnp
from jax import lax
from jax.sharding import PartitionSpec as P

ITERS = 2


def project(rows_block, matrix):
    return jnp.dot(rows_block.astype(jnp.float32), matrix, precision=lax.Precision.HIGHEST).astype(
        jnp.bfloat16
    )


def tile_costs(projected, cols_block):
    return -4.0 * lax.dot_general(
        projected, cols_block, (((1,), (1,)), ((), ())), preferred_element_type=jnp.float32
    )


def row_totals(scores):
    top_score = lax.pmax(jnp.max(scores, axis=1), "col")
    mass_total = lax.psum(jnp.sum(jnp.exp(scores - top_score[:, None]), axis=1), "col")
    return top_score + jnp.log(mass_total)


def column_totals(scores):
    top_score = lax.pmax(jnp.max(scores, axis=0), "row")
    mass_total = lax.psum(jnp.sum(jnp.exp(scores - top_score[None, :]), axis=0), "row")
    return top_score + jnp.log(mass_total)


def per_device(source, target, target_potential, prev_moment):
    rows_block = lax.all_gather(source, "col", axis=0, tiled=True)
    cols_block, potential = (
        lax.all_gather(target, "row", axis=0, tiled=True),
        lax.all_gather(target_potential, "row", axis=0, tiled=True),
    )
    row_devices = lax.axis_size("row")
    rows_total = rows_block.shape[0] * row_devices
    cols_total = cols_block.shape[0] * lax.axis_size("col")
    share_width = cols_block.shape[0] // row_devices
    position = lax.axis_index("row")
    column = potential.astype(jnp.float32)
    scores = column[None, :] - tile_costs(project(rows_block, prev_moment), cols_block)
    spread = row_totals(scores)
    weights = (jnp.exp(scores - spread[:, None]) / rows_total).astype(jnp.bfloat16)
    carried = jnp.dot(weights, cols_block, preferred_element_type=jnp.float32)
    partial_moment = lax.dot_general(
        rows_block.astype(jnp.float32),
        carried,
        (((0,), (0,)), ((), ())),
        precision=lax.Precision.HIGHEST,
    )
    moment = lax.psum(partial_moment, ("row", "col"))
    cost_tile = tile_costs(project(rows_block, moment), cols_block)
    source_potential = jnp.zeros((rows_block.shape[0],), jnp.float32)
    own_share = jnp.zeros((share_width,), jnp.float32)
    for iteration in range(ITERS):
        source_potential = math.log(cols_total) - row_totals(column[None, :] - cost_tile)
        column_scores = source_potential[:, None] - cost_tile
        column = math.log(rows_total) - column_totals(column_scores)
        own_share = lax.dynamic_slice_in_dim(column, position * share_width, share_width)
    return (moment, source_potential, own_share)


def solution(mesh):
    placed = (P(("row", "col"), None), P(("col", "row"), None), P(("col", "row")), P())
    return jax.shard_map(
        per_device,
        mesh=mesh,
        in_specs=placed,
        out_specs=(P(), P("row"), P(("col", "row"))),
        check_vma=False,
    )
```

profile of v0, /device:TPU:32, one launch (start us, length us, event | category | flops | bytes accessed | tf_op | source)
XLA Modules:
  0.0 979.2 jit_solution(412638877074749381)
XLA Ops:
  8.0 21.8 %all-gather = bf16[32,1,128]{2,1,0:T(2,128)(2,1)S(1)} all-gather(bf16[1,1,128]{2,1,0:T(2,128)(2,1)} %bitcast.20), channel_id=1, replica_groups=mesh['row'=32,'col'=8] {'row'}, dimensions={0}, use_global_device_ids=true | all-gather | bytes 8448 | tf_op jit(solution)/shard_map/all_gather | solution.py:38
  29.8 27.7 %all_gather.10 = bf16[1024,128]{1,0:T(8,128)(2,1)S(1)} all-gather(bf16[128,128]{1,0:T(8,128)(2,1)} %param.4), channel_id=1, replica_groups=mesh['row'=32,'col'=8] {'col'}, dimensions={0}, use_global_device_ids=true | all-gather | bytes 294912 | tf_op jit(solution)/shard_map/all_gather | solution.py:35
  61.0 8.3 fusion
  69.3 16.0 %pmax.35 = f32[1024]{0:T(1024)S(1)} all-reduce(f32[1024]{0:T(1024)S(1)} %get-tuple-element.9), channel_id=1, replica_groups=mesh['row'=32,'col'=8] {'col'}, use_global_device_ids=true, to_apply=%region_1.0 | all-reduce | flops 1024 | bytes 8192 | tf_op jit(solution)/shard_map/pmax | solution.py:23
  85.4 7.8 exponential_reduce_fusion.4
  93.2 16.0 %psum.42 = f32[1024]{0:T(1024)S(1)} all-reduce(f32[1024]{0:T(1024)S(1)} %exponential_reduce_fusion.4), channel_id=1, replica_groups=mesh['row'=32,'col'=8] {'col'}, use_global_device_ids=true, to_apply=%region_3.0 | all-reduce | flops 1024 | bytes 8192 | tf_op jit(solution)/shard_map/psum | solution.py:24
  109.2 7.8 fusion.1
  118.3 234.4 %all-reduce.2.cloned.1.call-done = f32[128,128]{0,1:T(8,128)} async-done(((f32[128,128]{0,1:T(8,128)}), f32[128,128]{0,1:T(8,128)}) %all-reduce.2.cloned.1.call-update) | async-done | bytes 65552 | tf_op jit(solution)/shard_map/psum | solution.py:56
  353.9 7.0 subtract_reduce_fusion.3
  360.9 15.2 %pmax.36 = f32[1024]{0:T(1024)S(1)} all-reduce(f32[1024]{0:T(1024)S(1)} %get-tuple-element.11), channel_id=1, replica_groups=mesh['row'=32,'col'=8] {'col'}, use_global_device_ids=true, to_apply=%region_6.0 | all-reduce | flops 1024 | bytes 8192 | tf_op jit(solution)/shard_map/pmax | solution.py:23
  376.1 7.8 exponential_reduce_fusion.3
  384.0 15.1 %psum.44 = f32[1024]{0:T(1024)S(1)} all-reduce(f32[1024]{0:T(1024)S(1)} %exponential_reduce_fusion.3), channel_id=1, replica_groups=mesh['row'=32,'col'=8] {'col'}, use_global_device_ids=true, to_apply=%region_8.0 | all-reduce | flops 1024 | bytes 8192 | tf_op jit(solution)/shard_map/psum | solution.py:24
  399.1 7.7 subtract_reduce_fusion.2
  406.8 124.0 %pmax.37 = f32[4096]{0:T(1024)S(1)} all-reduce(f32[4096]{0:T(1024)S(1)} %subtract_reduce_fusion.2), channel_id=1, replica_groups=mesh['row'=32,'col'=8] {'row'}, use_global_device_ids=true, to_apply=%region_10.0 | all-reduce | flops 4096 | bytes 32768 | tf_op jit(solution)/shard_map/pmax | solution.py:29
  530.8 7.7 exponential_reduce_fusion.2
  538.5 123.8 %psum.45 = f32[4096]{0:T(1024)S(1)} all-reduce(f32[4096]{0:T(1024)S(1)} %exponential_reduce_fusion.2), channel_id=1, replica_groups=mesh['row'=32,'col'=8] {'row'}, use_global_device_ids=true, to_apply=%region_12.0 | all-reduce | flops 4096 | bytes 32768 | tf_op jit(solution)/shard_map/psum | solution.py:30
  662.3 7.5 subtract_reduce_fusion.1
  669.8 15.2 %pmax.38 = f32[1024]{0:T(1024)S(1)} all-reduce(f32[1024]{0:T(1024)S(1)} %subtract_reduce_fusion.1), channel_id=1, replica_groups=mesh['row'=32,'col'=8] {'col'}, use_global_device_ids=true, to_apply=%region_14.0 | all-reduce | flops 1024 | bytes 8192 | tf_op jit(solution)/shard_map/pmax | solution.py:23
  685.0 7.8 exponential_reduce_fusion.1
  692.8 15.1 %psum.46 = f32[1024]{0:T(1024)S(1)} all-reduce(f32[1024]{0:T(1024)S(1)} %exponential_reduce_fusion.1), channel_id=1, replica_groups=mesh['row'=32,'col'=8] {'col'}, use_global_device_ids=true, to_apply=%region_16.0 | all-reduce | flops 1024 | bytes 8192 | tf_op jit(solution)/shard_map/psum | solution.py:24
  708.0 7.8 subtract_reduce_fusion
  715.7 123.8 %pmax.39 = f32[4096]{0:T(1024)S(1)} all-reduce(f32[4096]{0:T(1024)S(1)} %subtract_reduce_fusion), channel_id=1, replica_groups=mesh['row'=32,'col'=8] {'row'}, use_global_device_ids=true, to_apply=%region_18.0 | all-reduce | flops 4096 | bytes 32768 | tf_op jit(solution)/shard_map/pmax | solution.py:29
  839.5 7.7 exponential_reduce_fusion
  847.3 123.8 %psum.47 = f32[4096]{0:T(1024)S(1)} all-reduce(f32[4096]{0:T(1024)S(1)} %exponential_reduce_fusion), channel_id=1, replica_groups=mesh['row'=32,'col'=8] {'row'}, use_global_device_ids=true, to_apply=%region_20.0 | all-reduce | flops 4096 | bytes 32768 | tf_op jit(solution)/shard_map/psum | solution.py:30
  (23 shorter events, 8.1 us)
Async XLA Ops:
  7.2 50.3 %copy-start = (f32[128,128]{1,0:T(8,128)S(1)}, f32[128,128]{1,0:T(8,128)}, u32[]{:S(2)}) copy-start(f32[128,128]{1,0:T(8,128)} %param.7) | copy-start | bytes 196612
  7.2 53.8 %all-gather.3.cloned.1.call-start = ((), (), s32[]{:S(2)}) async-start(), calls=%async_computation | async-start | bytes 1081344 | tf_op jit(solution)/shard_map/all_gather | solution.py:37
  7.9 344.7 %all-reduce.2.cloned.1.call-start = ((), (), s32[]{:S(2)}) async-start(), calls=%async_computation.1 | async-start | bytes 131072 | tf_op jit(solution)/shard_map/psum | solution.py:56
  61.0 48.2 %copy-start.1 = (bf16[4096,128]{1,0:T(8,128)(2,1)S(1)}, bf16[4096,128]{1,0:T(8,128)(2,1)}, u32[]{:S(2)}) copy-start(bf16[4096,128]{1,0:T(8,128)(2,1)} %all-gather.3.cloned.1.call-done) | copy-start | bytes 3145732
  708.0 139.3 %copy-start.3 = (f32[1024]{0:T(1024)}, f32[1024]{0:T(1024)S(1)}, u32[]{:S(2)}) copy-start(f32[1024]{0:T(1024)S(1)} %add_subtract_fusion.1) | copy-start | bytes 12292
  708.0 263.7 %copy-start.2 = (f32[128,128]{0,1:T(8,128)S(1)}, f32[128,128]{0,1:T(8,128)}, u32[]{:S(2)}) copy-start(f32[128,128]{0,1:T(8,128)} %all-reduce.2.cloned.1.call-done) | copy-start | bytes 196612
Sparse Core Ops, SparseCore 0:
  10.6 50.3 all-gather.2
  118.4 234.2 all-reduce.1
where the time goes:
time: 980 us; the launch traced here: 979 us
  blocking collectives  638 us (65%)
  waiting for transfers between devices  238 us (24%)
  other arithmetic  62.6 us (6%)
  matrix products  25.9 us (3%)
  between operations  14.1 us (1%)
    pmax x2, blocking collectives, column_totals(): top_score = lax.pmax(jnp.max(scores, axis=0), 'row')  248 us
    psum x2, blocking collectives, column_totals(): lax.psum(jnp.sum(jnp.exp(scores - top_score[None, :]), axis=0), 'row')  248 us
    psum x1, waiting for transfers between devices, per_device(): moment = lax.psum(partial_moment, ('row', 'col'))  234 us
    pmax x3, blocking collectives, row_totals(): top_score = lax.pmax(jnp.max(scores, axis=1), 'col')  46.5 us
    psum x3, blocking collectives, row_totals(): lax.psum(jnp.sum(jnp.exp(scores - top_score[:, None]), axis=1), 'col')  46.2 us
    all_gather x1, blocking collectives, per_device(): rows_block = lax.all_gather(source, 'col', axis=0, tiled=True)  27.7 us
    reduce_sum x3, other arithmetic, row_totals(): jnp.sum(jnp.exp(scores - top_score[:, None]), axis=1)  23.5 us
    all_gather x1, blocking collectives, per_device(): lax.all_gather(target_potential, 'row', axis=0, tiled=True)  21.8 us
  transfers between devices with their start and end apart: 2, of which 2 were waited for; matrix products, arithmetic and copies ran while one was open for 0% of the time, Pallas kernels for 0%

commit v1 on v0

--- a/solution.py
+++ b/solution.py
@@ -5,6 +5,12 @@
 from jax.sharding import PartitionSpec as P
 
 ITERS = 2
+
+
+def add_all(x, mesh_axis):
+    pieces = lax.all_gather(x, mesh_axis, axis=0, tiled=False)
+    result = pieces.sum(axis=0)
+    return result
 
 
 def project(rows_block, matrix):
@@ -27,7 +33,7 @@
 
 def column_totals(scores):
     top_score = lax.pmax(jnp.max(scores, axis=0), "row")
-    mass_total = lax.psum(jnp.sum(jnp.exp(scores - top_score[None, :]), axis=0), "row")
+    mass_total = add_all(jnp.sum(jnp.exp(scores - top_score[None, :]), axis=0), "row")
     return top_score + jnp.log(mass_total)
 
 

time: 980 us -> 778 us (0.79)
  blocking collectives: 638 us -> 433 us
    psum x2 -> x0, blocking collectives: 248 us -> none  [column_totals(): lax.psum(jnp.sum(jnp.exp(scores - top_score[None, :]), axis=0), 'row')]
    all_gather x0 -> x2, blocking collectives: none -> 43.5 us  [add_all(): pieces = lax.all_gather(x, mesh_axis, axis=0, tiled=False)]
where the time goes in v1:
time: 778 us; the launch traced here: 776 us
  blocking collectives  433 us (56%)
  waiting for transfers between devices  238 us (31%)
  other arithmetic  62.7 us (8%)
  matrix products  25.9 us (3%)
  between operations  14.2 us (2%)
    pmax x2, blocking collectives, column_totals(): top_score = lax.pmax(jnp.max(scores, axis=0), 'row')  248 us
    psum x1, waiting for transfers between devices, per_device(): moment = lax.psum(partial_moment, ('row', 'col'))  234 us
    pmax x3, blocking collectives, row_totals(): top_score = lax.pmax(jnp.max(scores, axis=1), 'col')  46.5 us
    psum x3, blocking collectives, row_totals(): lax.psum(jnp.sum(jnp.exp(scores - top_score[:, None]), axis=1), 'col')  46.2 us
    all_gather x2, blocking collectives, add_all(): pieces = lax.all_gather(x, mesh_axis, axis=0, tiled=False)  43.5 us
    all_gather x1, blocking collectives, per_device(): rows_block = lax.all_gather(source, 'col', axis=0, tiled=True)  27.7 us
    reduce_sum x3, other arithmetic, row_totals(): jnp.sum(jnp.exp(scores - top_score[:, None]), axis=1)  23.5 us
    all_gather x1, blocking collectives, per_device(): lax.all_gather(target_potential, 'row', axis=0, tiled=True)  21.8 us
  transfers between devices with their start and end apart: 2, of which 2 were waited for; matrix products, arithmetic and copies ran while one was open for 0% of the time, Pallas kernels for 0%

profile of v1, /device:TPU:32, one launch (start us, length us, event | category | flops | bytes accessed | tf_op | source)
XLA Modules:
  0.0 775.5 jit_solution(6265074148045334683)
XLA Ops:
  8.0 21.8 %all-gather.2 = bf16[32,1,128]{2,1,0:T(2,128)(2,1)S(1)} all-gather(bf16[1,1,128]{2,1,0:T(2,128)(2,1)} %bitcast.20), channel_id=1, replica_groups=mesh['row'=32,'col'=8] {'row'}, dimensions={0}, use_global_device_ids=true | all-gather | bytes 8448 | tf_op jit(solution)/shard_map/all_gather | solution.py:44
  29.8 27.7 %all_gather.22 = bf16[1024,128]{1,0:T(8,128)(2,1)S(1)} all-gather(bf16[128,128]{1,0:T(8,128)(2,1)} %param.4), channel_id=1, replica_groups=mesh['row'=32,'col'=8] {'col'}, dimensions={0}, use_global_device_ids=true | all-gather | bytes 294912 | tf_op jit(solution)/shard_map/all_gather | solution.py:41
  61.0 8.3 %fusion = (f32[1024]{0:T(1024)S(1)}, f32[1024,4096]{1,0:T(8,128)}) fusion(f32[4096]{0:T(1024)S(1)} %bitcast.15, bf16[1024,128]{1,0:T(8,128)(2,1)S(1)} %convolution_convert_fusion.1, bf16[4096,128]{1,0:T(8,128)(2,1)} %all-gather.5.cloned.1.call-done), kind=kOutput, calls=%fused_computation.11 | convolution fusion | flops 1086323712 | bytes 18108416 | tf_op jit(solution)/shard_map/dot_general | solution.py:23
  69.3 16.0 %pmax.35 = f32[1024]{0:T(1024)S(1)} all-reduce(f32[1024]{0:T(1024)S(1)} %get-tuple-element.12), channel_id=1, replica_groups=mesh['row'=32,'col'=8] {'col'}, use_global_device_ids=true, to_apply=%region_1.0 | all-reduce | flops 1024 | bytes 8192 | tf_op jit(solution)/shard_map/pmax | solution.py:29
  85.4 7.8 %exponential_reduce_fusion.4 = f32[1024]{0:T(1024)S(1)} fusion(f32[1024,4096]{1,0:T(8,128)} %get-tuple-element.13, f32[1024]{0:T(1024)S(1)} %pmax.35, f32[4096]{0:T(1024)S(1)} %bitcast.16), kind=kLoop, calls=%fused_computation.5 | loop fusion | flops 16776192 | bytes 16801792 | tf_op jit(solution)/shard_map/reduce_sum | solution.py:30
  93.2 16.0 %psum.28 = f32[1024]{0:T(1024)S(1)} all-reduce(f32[1024]{0:T(1024)S(1)} %exponential_reduce_fusion.4), channel_id=1, replica_groups=mesh['row'=32,'col'=8] {'col'}, use_global_device_ids=true, to_apply=%region_3.0 | all-reduce | flops 1024 | bytes 8192 | tf_op jit(solution)/shard_map/psum | solution.py:30
  109.2 7.8 %fusion.1 = f32[1024,128]{1,0:T(8,128)S(1)} fusion(bf16[4096,128]{1,0:T(8,128)(2,1)S(1)} %copy-done.1, f32[1024,4096]{1,0:T(8,128)} %get-tuple-element.13, f32[1024]{0:T(1024)S(1)} %log_add_fusion, f32[4096]{0:T(1024)S(1)} %bitcast.17), kind=kOutput, calls=%fused_computation.12 | convolution fusion | flops 1094713344 | bytes 18370560 | tf_op jit(solution)/shard_map/dot_general | solution.py:55
  118.3 234.4 %all-reduce.2.cloned.1.call-done = f32[128,128]{0,1:T(8,128)} async-done(((f32[128,128]{0,1:T(8,128)}), f32[128,128]{0,1:T(8,128)}) %all-reduce.2.cloned.1.call-update) | async-done | bytes 65552 | tf_op jit(solution)/shard_map/psum | solution.py:62
  353.9 7.0 subtract_reduce_fusion.3
  360.9 15.2 %pmax.36 = f32[1024]{0:T(1024)S(1)} all-reduce(f32[1024]{0:T(1024)S(1)} %get-tuple-element.14), channel_id=1, replica_groups=mesh['row'=32,'col'=8] {'col'}, use_global_device_ids=true, to_apply=%region_6.0 | all-reduce | flops 1024 | bytes 8192 | tf_op jit(solution)/shard_map/pmax | solution.py:29
  376.1 7.8 %exponential_reduce_fusion.3 = f32[1024]{0:T(1024)S(1)} fusion(f32[1024,4096]{1,0:T(8,128)} %get-tuple-element.15, f32[1024]{0:T(1024)S(1)} %pmax.36, f32[4096]{0:T(1024)S(1)} %bitcast.19), kind=kLoop, calls=%fused_computation.3 | loop fusion | flops 16776192 | bytes 16801792 | tf_op jit(solution)/shard_map/reduce_sum | solution.py:30
  384.0 15.1 %psum.30 = f32[1024]{0:T(1024)S(1)} all-reduce(f32[1024]{0:T(1024)S(1)} %exponential_reduce_fusion.3), channel_id=1, replica_groups=mesh['row'=32,'col'=8] {'col'}, use_global_device_ids=true, to_apply=%region_8.0 | all-reduce | flops 1024 | bytes 8192 | tf_op jit(solution)/shard_map/psum | solution.py:30
  399.1 7.7 subtract_reduce_fusion.2
  406.8 124.0 %pmax.37 = f32[4096]{0:T(1024)S(1)} all-reduce(f32[4096]{0:T(1024)S(1)} %subtract_reduce_fusion.2), channel_id=1, replica_groups=mesh['row'=32,'col'=8] {'row'}, use_global_device_ids=true, to_apply=%region_10.0 | all-reduce | flops 4096 | bytes 32768 | tf_op jit(solution)/shard_map/pmax | solution.py:35
  530.8 7.7 exponential_reduce_fusion.2
  538.5 21.8 %all-gather = f32[131072]{0:T(1024)S(1)} all-gather(f32[4096]{0:T(1024)S(1)} %exponential_reduce_fusion.2), channel_id=2, replica_groups=mesh['row'=32,'col'=8] {'row'}, dimensions={0}, use_global_device_ids=true | all-gather | bytes 540672 | tf_op jit(solution)/shard_map/all_gather | solution.py:11
  560.5 7.5 subtract_reduce_fusion.1
  567.9 15.2 %pmax.38 = f32[1024]{0:T(1024)S(1)} all-reduce(f32[1024]{0:T(1024)S(1)} %subtract_reduce_fusion.1), channel_id=1, replica_groups=mesh['row'=32,'col'=8] {'col'}, use_global_device_ids=true, to_apply=%region_14.0 | all-reduce | flops 1024 | bytes 8192 | tf_op jit(solution)/shard_map/pmax | solution.py:29
  583.2 7.8 %exponential_reduce_fusion.1 = f32[1024]{0:T(1024)S(1)} fusion(f32[1024,4096]{1,0:T(8,128)} %get-tuple-element.15, f32[1024]{0:T(1024)S(1)} %pmax.38, f32[4096]{0:T(1024)S(1)} %add_subtract_fusion), kind=kLoop, calls=%fused_computation.1 | loop fusion | flops 16776192 | bytes 16801792 | tf_op jit(solution)/shard_map/reduce_sum | solution.py:30
  591.0 15.1 %psum.31 = f32[1024]{0:T(1024)S(1)} all-reduce(f32[1024]{0:T(1024)S(1)} %exponential_reduce_fusion.1), channel_id=1, replica_groups=mesh['row'=32,'col'=8] {'col'}, use_global_device_ids=true, to_apply=%region_16.0 | all-reduce | flops 1024 | bytes 8192 | tf_op jit(solution)/shard_map/psum | solution.py:30
  606.1 7.8 %subtract_reduce_fusion = f32[4096]{0:T(1024)S(1)} fusion(f32[1024,4096]{1,0:T(8,128)} %get-tuple-element.15, f32[1024]{0:T(1024)S(1)} %add_subtract_fusion.1), kind=kLoop, calls=%fused_computation.7 | loop fusion | flops 12578816 | bytes 16797696 | tf_op jit(solution)/shard_map/reduce_max | solution.py:35
  613.9 123.8 %pmax.39 = f32[4096]{0:T(1024)S(1)} all-reduce(f32[4096]{0:T(1024)S(1)} %subtract_reduce_fusion), channel_id=1, replica_groups=mesh['row'=32,'col'=8] {'row'}, use_global_device_ids=true, to_apply=%region_18.0 | all-reduce | flops 4096 | bytes 32768 | tf_op jit(solution)/shard_map/pmax | solution.py:35
  737.7 7.7 exponential_reduce_fusion
  745.4 21.8 %all-gather.1 = f32[131072]{0:T(1024)S(1)} all-gather(f32[4096]{0:T(1024)S(1)} %exponential_reduce_fusion), channel_id=3, replica_groups=mesh['row'=32,'col'=8] {'row'}, dimensions={0}, use_global_device_ids=true | all-gather | bytes 540672 | tf_op jit(solution)/shard_map/all_gather | solution.py:11
  (27 shorter events, 8.4 us)
Async XLA Ops:
  7.2 50.3 %copy-start = (f32[128,128]{1,0:T(8,128)S(1)}, f32[128,128]{1,0:T(8,128)}, u32[]{:S(2)}) copy-start(f32[128,128]{1,0:T(8,128)} %param.7) | copy-start | bytes 196612
  7.2 53.8 %all-gather.5.cloned.1.call-start = ((), (), s32[]{:S(2)}) async-start(), calls=%async_computation | async-start | bytes 1081344 | tf_op jit(solution)/shard_map/all_gather | solution.py:43
  7.9 344.7 %all-reduce.2.cloned.1.call-start = ((), (), s32[]{:S(2)}) async-start(), calls=%async_computation.1 | async-start | bytes 131072 | tf_op jit(solution)/shard_map/psum | solution.py:62
  61.0 48.2 %copy-start.1 = (bf16[4096,128]{1,0:T(8,128)(2,1)S(1)}, bf16[4096,128]{1,0:T(8,128)(2,1)}, u32[]{:S(2)}) copy-start(bf16[4096,128]{1,0:T(8,128)(2,1)} %all-gather.5.cloned.1.call-done) | copy-start | bytes 3145732
  606.1 139.3 %copy-start.3 = (f32[1024]{0:T(1024)}, f32[1024]{0:T(1024)S(1)}, u32[]{:S(2)}) copy-start(f32[1024]{0:T(1024)S(1)} %add_subtract_fusion.1) | copy-start | bytes 12292
  606.1 161.8 %copy-start.2 = (f32[128,128]{0,1:T(8,128)S(1)}, f32[128,128]{0,1:T(8,128)}, u32[]{:S(2)}) copy-start(f32[128,128]{0,1:T(8,128)} %all-reduce.2.cloned.1.call-done) | copy-start | bytes 196612
Sparse Core Ops, SparseCore 0:
  10.6 50.3 all-gather.4
  118.4 234.2 all-reduce.1
